TPU v7x, 512 devices: a whole 4x8x8 slice. The times are simulated.
512 devices in a mesh: dp: 16 (over z_hi, y), context: 32 (over z_lo, x, core).
Axes of the slice: x: 4, y: 8, z: 8 (z_hi: 2, z_lo: 4; z = z_hi * 4 + z_lo), core: 2. Of those that a mesh axis runs over, the one named last changes fastest.
Arguments:
- values: float32 [16, 256, 4096], P('dp', None, 'context'), may hold values from -6 to 6
- in_gate: float32 [16, 256, 4096], P('dp', None, 'context'), may hold values from -6 to 6
- out_gate: float32 [16, 256, 4096], P('dp', None, 'context'), may hold values from -6 to 6
- target: float32 [16, 256, 4096], P('dp', None, 'context'), may hold values from -6 to 6
- tap_param: float32 [256, 4096], P('context', 'dp'), may hold values from -6 to 6
- skip: float32 [256], replicated, may hold values from 0.1 to 1.9
Outputs:
- grad_values: float32 [16, 256, 4096], P('dp', None, 'context')
- tap_grad: float32 [256, 4096], P('context', 'dp')
All inputs are finite; a program needn't handle non-finite values.
Results may differ from a plain program's by a relative error of at most 0.0003.
Values sent between devices are 32-bit elements; how exact they have to be, the bound alone decides.
A program may use at most 64 MiB of HBM per device.

v0:
```python
import math

import jax
import jax.numpy as jnp
from jax import lax
from jax.sharding import PartitionSpec as P


def matmul_high(left, right):
    return jnp.matmul(left, right, precision=lax.Precision.HIGHEST)


def direct(real_part, imag_part, orient):
    length = real_part.shape[-1]
    counter = jnp.arange(length, dtype=jnp.int32)
    products = counter[:, None] * counter[None, :] % length
    angles = 2.0 * math.pi / length * products.astype(jnp.float32)
    cosine = jnp.cos(angles)
    sine = orient * jnp.sin(angles)
    matrix = jnp.concatenate(
        [jnp.concatenate([cosine, sine], axis=1), jnp.concatenate([-sine, cosine], axis=1)], axis=0
    )
    joined = jnp.concatenate([real_part, imag_part], axis=-1)
    result = matmul_high(joined, matrix)
    return (result[..., :length], result[..., length:])


def transform(real_part, imag_part, orient):
    length = real_part.shape[-1]
    if length <= 128:
        return direct(real_part, imag_part, orient)
    radix_a = 128
    remain = length // radix_a
    leading = real_part.shape[:-1]

    def split_axes(signal):
        return jnp.swapaxes(signal.reshape(leading + (remain, radix_a)), -1, -2)

    inner_real, inner_imag = transform(split_axes(real_part), split_axes(imag_part), orient)
    first_index = jnp.arange(radix_a, dtype=jnp.int32)
    second_index = jnp.arange(remain, dtype=jnp.int32)
    products = first_index[:, None] * second_index[None, :] % length
    angles = 2.0 * math.pi / length * products.astype(jnp.float32)
    twiddle_cos = jnp.cos(angles)
    twiddle_sin = orient * jnp.sin(angles)
    turned_real = inner_real * twiddle_cos - inner_imag * twiddle_sin
    turned_imag = inner_real * twiddle_sin + inner_imag * twiddle_cos
    outer_real, outer_imag = direct(
        jnp.swapaxes(turned_real, -1, -2), jnp.swapaxes(turned_imag, -1, -2), orient
    )
    final_real = jnp.swapaxes(outer_real, -1, -2).reshape(leading + (length,))
    final_imag = jnp.swapaxes(outer_imag, -1, -2).reshape(leading + (length,))
    return (final_real, final_imag)


def spectrum(signal):
    length = signal.shape[-1]
    padded = jnp.pad(signal, [(0, 0)] * (signal.ndim - 1) + [(0, length)])
    return transform(padded, jnp.zeros_like(padded), -1.0)


def complex_mul(left, right):
    return (left[0] * right[0] - left[1] * right[1], left[0] * right[1] + left[1] * right[0])


def conj_mul(left, right):
    return (left[0] * right[0] + left[1] * right[1], left[1] * right[0] - left[0] * right[1])


def inverse_real(spec, length):
    out_real, out_imag = transform(spec[0], spec[1], 1.0)
    return out_real[..., :length] / (2.0 * length)


def backward(grad_spec, tap_spec, mixed_spec, length):
    first_term = conj_mul(grad_spec, tap_spec)
    second_term = conj_mul(grad_spec, mixed_spec)
    return (inverse_real(first_term, length), inverse_real(second_term, length))


def body(values, in_gate, out_gate, target, tap_param, skip):
    taps_full = lax.all_gather(tap_param, "dp", axis=1, tiled=True)
    seq_len = taps_full.shape[1]
    taps = taps_full * seq_len ** (-0.5)
    mixed = values * in_gate
    tap_spec = spectrum(taps)
    mixed_cols = lax.all_to_all(mixed, "context", split_axis=1, concat_axis=2, tiled=True)
    mixed_spec = spectrum(mixed_cols)
    conv = inverse_real(complex_mul(mixed_spec, tap_spec), seq_len)
    conv_tok = lax.all_to_all(conv, "context", split_axis=2, concat_axis=1, tiled=True)
    skip_tok = skip[None, :, None]
    middle = conv_tok + skip_tok * mixed
    grad_out = out_gate * (out_gate * middle - target)
    grad_cols = lax.all_to_all(grad_out, "context", split_axis=1, concat_axis=2, tiled=True)
    grad_spec = spectrum(grad_cols)
    back_cols, tap_raw = backward(grad_spec, tap_spec, mixed_spec, seq_len)
    back_tok = lax.all_to_all(back_cols, "context", split_axis=2, concat_axis=1, tiled=True)
    grad_values = in_gate * (back_tok + skip_tok * grad_out)
    batch_all = values.shape[0] * lax.axis_size("dp")
    tap_local = jnp.sum(tap_raw, axis=0) * (seq_len * batch_all) ** (-0.5)
    tap_grad = lax.psum_scatter(tap_local, "dp", scatter_dimension=1, tiled=True)
    return (grad_values, tap_grad)


def solution(mesh):
    placed = (
        P("dp", None, "context"),
        P("dp", None, "context"),
        P("dp", None, "context"),
        P("dp", None, "context"),
        P("context", "dp"),
        P(),
    )
    return jax.shard_map(
        body,
        mesh=mesh,
        in_specs=placed,
        out_specs=(P("dp", None, "context"), P("context", "dp")),
        check_vma=False,
    )
```

profile of v0, /device:TPU:6, one launch (start us, length us, event | category | flops | bytes accessed | tf_op | source)
XLA Modules:
  0.0 402.6 jit_solution(1416449022692591965)
XLA Ops:
  7.2 1.6 mul.912
  8.8 10.4 %all-to-all-start = ((f32[1,256,128]{2,0,1:T(1,128)}), f32[1,256,128]{2,0,1:T(1,128)S(1)}, u32[]{:S(2)}, u32[]{:S(2)}) async-start(f32[1,256,128]{2,0,1:T(1,128)} %bitcast), calls=%async_computation | async-start | bytes 262144 | tf_op jit(solution)/shard_map/all_to_all | solution.py:87
  20.2 55.7 %all_gather.3 = f32[8,4096]{1,0:T(8,128)S(1)} all-gather(f32[8,256]{1,0:T(8,128)} %param.10), channel_id=1, replica_groups=mesh['dp'=16,'context'=32] {'dp'}, dimensions={1}, use_global_device_ids=true | all-gather | bytes 139264 | tf_op jit(solution)/shard_map/all_gather | solution.py:82
  76.2 0.6 fusion.23
  79.4 0.6 convolution_bitcast_fusion.9
  80.1 0.6 convolution_bitcast_fusion.8
  81.6 0.6 convolution_bitcast_fusion.7
  82.3 0.6 convolution_bitcast_fusion.6
  83.3 2.6 copy.105
  86.5 19.3 %reduce = f32[4096,8]{1,0:T(8,128)} reduce(f32[4096,1,8]{2,1,0:T(1,128)S(1)} %bitcast.182, f32[]{:T(128)} %broadcast.287), dimensions={1}, to_apply=%bitcast.177.reduce_sub_computation | reduce | bytes 262148
  105.7 2.7 reshape.487
  108.5 13.9 %all_to_all.72 = f32[32,1,1024]{2,1,0:T(1,128)S(1)} all-to-all(f32[32,1,1024]{2,1,0:T(1,128)S(1)} %reshape.487), channel_id=1, replica_groups=mesh['dp'=16,'context'=32] {'context'}, dimensions={0} | all-to-all | bytes 262144 | tf_op jit(solution)/shard_map/all_to_all | solution.py:90
  122.4 0.8 reduce.1
  123.3 3.5 reshape.488
  126.8 1.2 copy.106
  128.0 1.2 fusion.40
  129.2 12.3 %all_to_all.73 = f32[1,256,128]{2,0,1:T(1,128)S(1)} all-to-all(f32[1,256,128]{2,0,1:T(1,128)S(1)} %bitcast.189), channel_id=1, replica_groups=mesh['dp'=16,'context'=32] {'context'}, dimensions={1} | all-to-all | bytes 262144 | tf_op jit(solution)/shard_map/all_to_all | solution.py:94
  141.9 0.6 convolution_bitcast_fusion.5
  142.7 0.6 convolution_bitcast_fusion.4
  144.5 0.6 convolution_bitcast_fusion.1
  145.1 0.6 convolution_bitcast_fusion.3
  145.9 0.6 convolution_bitcast_fusion
  148.0 2.5 copy.114
  150.4 19.3 %reduce.2 = f32[4096,8]{1,0:T(8,128)} reduce(f32[4096,1,8]{2,1,0:T(1,128)S(1)} %bitcast.184, f32[]{:T(128)} %broadcast.287), dimensions={1}, to_apply=%bitcast.179.reduce_sub_computation | reduce | bytes 262148
  169.7 3.3 reshape.489
  173.0 5.7 %all-to-all-start.3 = ((f32[32,1,1024]{2,1,0:T(1,128)}), f32[32,1,1024]{2,1,0:T(1,128)S(1)}, u32[]{:S(2)}, u32[]{:S(2)}) async-start(f32[32,1,1024]{2,1,0:T(1,128)} %reshape.489), calls=%async_computation.3 | async-start | bytes 262144 | tf_op jit(solution)/shard_map/all_to_all | solution.py:97
  179.1 0.7 fusion.36
  179.8 5.8 %all-to-all-done.3 = f32[32,1,1024]{2,1,0:T(1,128)S(1)} async-done(((f32[32,1,1024]{2,1,0:T(1,128)}), f32[32,1,1024]{2,1,0:T(1,128)S(1)}, u32[]{:S(2)}, u32[]{:S(2)}) %all-to-all-start.3) | async-done | bytes 131104 | tf_op jit(solution)/shard_map/all_to_all | solution.py:97
  185.6 0.8 reduce.3
  186.5 3.5 reshape.490
  190.6 0.8 fusion.37
  191.3 204.4 %reduce-scatter.2.cloned.1.call-done = f32[8,256]{1,0:T(8,128)} async-done(((f32[8,4096]{1,0:T(8,128)}), f32[8,256]{1,0:T(8,128)}) %reduce-scatter.2.cloned.1.call-update) | async-done | bytes 8208 | tf_op jit(solution)/shard_map/reduce_scatter | solution.py:101
  (94 shorter events, 9.5 us)
Async XLA Ops:
  8.8 70.1 %all-to-all-start = ((f32[1,256,128]{2,0,1:T(1,128)}), f32[1,256,128]{2,0,1:T(1,128)S(1)}, u32[]{:S(2)}, u32[]{:S(2)}) async-start(f32[1,256,128]{2,0,1:T(1,128)} %bitcast), calls=%async_computation | async-start | bytes 262144 | tf_op jit(solution)/shard_map/all_to_all | solution.py:87
  19.3 60.0 %copy-start.4 = (f32[64,64]{0,1:T(8,128)}, f32[64,64]{0,1:T(8,128)S(1)}, u32[]{:S(2)}) copy-start(f32[64,64]{0,1:T(8,128)S(1)} %fusion.72) | copy-start | bytes 49156
  19.6 60.5 %copy-start = (f32[128,128]{1,0:T(8,128)}, f32[128,128]{1,0:T(8,128)S(1)}, u32[]{:S(2)}) copy-start(f32[128,128]{1,0:T(8,128)S(1)} %fusion.66) | copy-start | bytes 196612
  19.8 59.6 %copy-start.8 = (f32[64,64]{0,1:T(8,128)}, f32[64,64]{0,1:T(8,128)S(1)}, u32[]{:S(2)}) copy-start(f32[64,64]{0,1:T(8,128)S(1)} %get-tuple-element.32) | copy-start | bytes 49156
  19.9 60.1 %copy-start.6 = (f32[128,64]{0,1:T(8,128)}, f32[128,64]{0,1:T(8,128)S(1)}, u32[]{:S(2)}) copy-start(f32[128,64]{0,1:T(8,128)S(1)} %get-tuple-element.34) | copy-start | bytes 98308
  20.2 59.9 %copy-start.2 = (f32[128,128]{1,0:T(8,128)}, f32[128,128]{1,0:T(8,128)S(1)}, u32[]{:S(2)}) copy-start(f32[128,128]{1,0:T(8,128)S(1)} %get-tuple-element.36) | copy-start | bytes 196612
  77.8 4.5 %copy-start.15 = (f32[128,64]{0,1:T(8,128)}, f32[128,64]{0,1:T(8,128)S(1)}, u32[]{:S(2)}) copy-start(f32[128,64]{0,1:T(8,128)S(1)} %fusion.67) | copy-start | bytes 98308
  78.6 2.9 copy-start.10
  78.6 2.9 copy-start.12
  123.2 4.8 %copy-start.17 = (f32[256]{0:T(256)S(1)}, f32[256]{0:T(256)}, u32[]{:S(2)}) copy-start(f32[256]{0:T(256)} %param.11) | copy-start | bytes 3076
  128.0 13.9 %copy-start.5 = (f32[64,64]{0,1:T(8,128)S(1)}, f32[64,64]{0,1:T(8,128)}, u32[]{:S(2)}) copy-start(f32[64,64]{0,1:T(8,128)} %copy-done.4) | copy-start | bytes 49156
  128.0 13.9 %copy-start.9 = (f32[64,64]{0,1:T(8,128)S(1)}, f32[64,64]{0,1:T(8,128)}, u32[]{:S(2)}) copy-start(f32[64,64]{0,1:T(8,128)} %copy-done.8) | copy-start | bytes 49156
  128.0 14.6 %copy-start.7 = (f32[128,64]{0,1:T(8,128)S(1)}, f32[128,64]{0,1:T(8,128)}, u32[]{:S(2)}) copy-start(f32[128,64]{0,1:T(8,128)} %copy-done.6) | copy-start | bytes 98308
  129.2 13.5 %copy-start.1 = (f32[128,128]{1,0:T(8,128)S(1)}, f32[128,128]{1,0:T(8,128)}, u32[]{:S(2)}) copy-start(f32[128,128]{1,0:T(8,128)} %copy-done) | copy-start | bytes 196612
  129.2 13.5 %copy-start.3 = (f32[128,128]{1,0:T(8,128)S(1)}, f32[128,128]{1,0:T(8,128)}, u32[]{:S(2)}) copy-start(f32[128,128]{1,0:T(8,128)} %copy-done.2) | copy-start | bytes 196612
  143.7 0.8 copy-start.11
  143.7 0.8 copy-start.13
  144.1 1.7 copy-start.16
  173.0 12.6 %all-to-all-start.3 = ((f32[32,1,1024]{2,1,0:T(1,128)}), f32[32,1,1024]{2,1,0:T(1,128)S(1)}, u32[]{:S(2)}, u32[]{:S(2)}) async-start(f32[32,1,1024]{2,1,0:T(1,128)} %reshape.489), calls=%async_computation.3 | async-start | bytes 262144 | tf_op jit(solution)/shard_map/all_to_all | solution.py:97
  178.8 217.0 %reduce-scatter.2.cloned.1.call-start = ((), (), s32[]{:S(2)}) async-start(), calls=%async_computation.5 | async-start | bytes 139264 | tf_op jit(solution)/shard_map/reduce_scatter | solution.py:101
  186.5 4.1 %copy-start.14 = (f32[1,256,128]{2,1,0:T(8,128)S(1)}, f32[1,256,128]{2,1,0:T(8,128)}, u32[]{:S(2)}) copy-start(f32[1,256,128]{2,1,0:T(8,128)} %param.7) | copy-start | bytes 393220
Sparse Core Ops, SparseCore 0:
  184.6 211.0 reduce-scatter.1
where the time goes:
time: 403 us
  waiting for transfers between devices  210 us (52%)
  blocking collectives  81.9 us (20%)
  other arithmetic  46.7 us (12%)
  local copies, waits for them, and re-layouts  25.2 us (6%)
  starting transfers between devices  16.4 us (4%)
  between operations  14.8 us (4%)
  matrix products  7.33 us (2%)
    reduce_scatter x1, waiting for transfers between devices, body(): lax.psum_scatter(tap_local, 'dp', scatter_dimension=1, tiled=True)  204 us
    all_gather x1, blocking collectives, body(): taps_full = lax.all_gather(tap_param, 'dp', axis=1, tiled=True)  55.7 us
    unnamed x2, other arithmetic  38.5 us
    unnamed x43, local copies, waits for them, and re-layouts  13.9 us
    all_to_all x1, blocking collectives, body(): lax.all_to_all(conv, 'context', split_axis=2, concat_axis=1, tiled=True)  13.9 us
    all_to_all x1, blocking collectives, body(): lax.all_to_all(grad_out, 'context', split_axis=1, concat_axis=2, tiled=True)  12.3 us
    all_to_all x1, starting transfers between devices, body(): lax.all_to_all(mixed, 'context', split_axis=1, concat_axis=2, tiled=True)  10.4 us
  transfers between devices with their start and end apart: 3, of which 2 were waited for; matrix products, arithmetic and copies ran while one was open for 3% of the time, Pallas kernels for 0%

commit v1 on v0

v1 whole, which is shorter than its diff:
```python
import functools
import math

import jax
import jax.numpy as jnp
import numpy as np
from jax import lax
from jax.experimental import pallas as pl
from jax.experimental.pallas import tpu as pltpu
from jax.sharding import PartitionSpec as P

MESH = pl.DeviceIdType.MESH
NB = 32
LANES = 128
CPD = 8
NY = 8
SEQ = NB * LANES
TAPS = 2 * LANES


def leaf_angles(theta, length):
    if length == 1:
        return [theta]
    return leaf_angles(theta / 2, length // 2) + leaf_angles(theta / 2 + math.pi, length // 2)


@functools.cache
def tables():
    order = np.array([round((a * 64 / (2 * math.pi) - 0.5) / 2) % NB for a in leaf_angles(math.pi / 2, NB)])
    r = np.arange(LANES)
    angle = 2 * math.pi * (2 * order[:, None] + 0.5) * r[None, :] / (2 * SEQ)
    turn = 2 * math.pi * (r[:, None] * r[None, :] % LANES) / LANES
    c, s = np.cos(turn), np.sin(turn)
    w = np.block([[c, -s], [s, c]]).astype(np.float32)
    w_hi = w.astype(jnp.bfloat16)
    w_lo = (w - w_hi.astype(np.float32)).astype(jnp.bfloat16)
    return (
        np.cos(angle).astype(np.float32)[:, None, :],
        np.sin(angle).astype(np.float32)[:, None, :],
        w_hi,
        w_lo,
    )


def evaluate(re, im, theta):
    length = re.shape[0]
    if length == 1:
        return [(re, im)]
    half = length // 2
    c, s = math.cos(theta / 2), math.sin(theta / 2)
    if im is None:
        t_re, t_im = c * re[half:], -s * re[half:]
        low = (re[:half] + t_re, t_im)
        high = (re[:half] - t_re, -t_im)
    else:
        t_re = c * re[half:] + s * im[half:]
        t_im = c * im[half:] - s * re[half:]
        low = (re[:half] + t_re, im[:half] + t_im)
        high = (re[:half] - t_re, im[:half] - t_im)
    return evaluate(*low, theta / 2) + evaluate(*high, theta / 2 + math.pi)


def gather_back(re, im, theta, real_only):
    length = re.shape[0]
    if length == 1:
        return re, im
    half = length // 2
    a_re, a_im = gather_back(re[:half], im[:half], theta / 2, False)
    b_re, b_im = gather_back(re[half:], im[half:], theta / 2 + math.pi, False)
    c, s = math.cos(theta / 2), math.sin(theta / 2)
    d_re, d_im = a_re - b_re, a_im - b_im
    top = c * d_re - s * d_im
    if real_only:
        return jnp.concatenate([a_re + b_re, top], axis=0), None
    return jnp.concatenate([a_re + b_re, top], axis=0), jnp.concatenate([a_im + b_im, c * d_im + s * d_re], axis=0)


def lane_transform(left, right, w_hi, w_lo):
    joined = jnp.concatenate([left, right], axis=1)
    hi = joined.astype(jnp.bfloat16)
    lo = (joined - hi.astype(jnp.float32)).astype(jnp.bfloat16)
    dot = functools.partial(jnp.dot, preferred_element_type=jnp.float32)
    out = dot(hi, w_hi[...]) + (dot(lo, w_hi[...]) + dot(hi, w_lo[...]))
    return out[:, :LANES], out[:, LANES:]


def forward(x, tcos, tsin, w_hi, w_lo):
    leaves = evaluate(x, None, math.pi / 2)
    re = jnp.concatenate([leaf[0] for leaf in leaves], axis=0)
    im = jnp.concatenate([leaf[1] for leaf in leaves], axis=0)
    c, s = tcos[...], tsin[...]
    flat = (NB * CPD, LANES)
    return lane_transform((re * c + im * s).reshape(flat), (im * c - re * s).reshape(flat), w_hi, w_lo)


def inverse(re, im, tcos, tsin, w_hi, w_lo):
    b_im, b_re = lane_transform(im, re, w_hi, w_lo)
    b_im, b_re = b_im.reshape(NB, CPD, LANES), b_re.reshape(NB, CPD, LANES)
    c, s = tcos[...], tsin[...]
    return gather_back(b_re * c - b_im * s, b_im * c + b_re * s, math.pi / 2, True)[0]


def conj_mul(a, b):
    return a[0] * b[0] + a[1] * b[1], a[1] * b[0] - a[0] * b[1]


def kernel(
    values, in_gate, out_gate, target, tap_param, skip, tcos_h, tsin_h, whi_h, wlo_h,
    grad_values, tap_grad,
    v_val, v_gate, tcos, tsin, w_hi, w_lo,
    mix_send, mix, gate, goal, taps, conv, back_send, back, tap_send, tap_recv, pair_send, pair_recv,
    load_sem, send_sem, recv_sem,
):
    me_d, me = lax.axis_index("dp"), lax.axis_index("context")
    mz, my = me_d // NY, me_d % NY

    loads = [(values.at[0], v_val), (in_gate.at[0], v_gate), (tcos_h, tcos), (tsin_h, tsin), (whi_h, w_hi), (wlo_h, w_lo)]
    loads = [pltpu.make_async_copy(src, dst, load_sem.at[k]) for k, (src, dst) in enumerate(loads)]
    own_rows = pl.ds(pl.multiple_of(me * CPD, CPD), CPD)
    loads += [
        pltpu.make_async_copy(out_gate.at[0, own_rows], gate.at[me], load_sem.at[6]),
        pltpu.make_async_copy(target.at[0, own_rows], goal.at[me], load_sem.at[7]),
        pltpu.make_async_copy(tap_param, taps.at[mz, my], load_sem.at[8]),
    ]
    for load in loads:
        load.start()

    barrier = pltpu.get_barrier_semaphore()

    def greet(s, carry):
        pl.semaphore_signal(barrier, inc=1, device_id=(me_d, (me + s) % NB), device_id_type=MESH)
        return carry

    def greet_y(s, carry):
        pl.semaphore_signal(barrier, inc=1, device_id=(mz * NY + (my + s) % NY, me), device_id_type=MESH)
        return carry

    lax.fori_loop(1, NB, greet, 0)
    lax.fori_loop(1, NY, greet_y, 0)
    pair = (1 - mz) * NY + my
    pl.semaphore_signal(barrier, inc=1, device_id=(pair, me), device_id_type=MESH)
    pl.semaphore_wait(barrier, NB - 1 + NY - 1 + 1)

    def remote(src, dst, k, device):
        return pltpu.make_async_remote_copy(
            src_ref=src, dst_ref=dst, send_sem=send_sem.at[k], recv_sem=recv_sem.at[k], device_id=device, device_id_type=MESH
        )

    def whole(ref, k):
        return remote(ref, ref, k, (me_d, (me + 1) % NB))

    def rows(p):
        return pl.ds(pl.multiple_of(p * CPD, CPD), CPD)

    def spread(make, k):
        def step(s, carry):
            p = (me + s) % NB
            src, dst = make(p)
            remote(src, dst, k, (me_d, p)).start()
            return carry

        lax.fori_loop(1, NB, step, 0)

    def spread_y(make, k):
        def step(s, carry):
            y = (my + s) % NY
            src, dst = make(y)
            remote(src, dst, k, (mz * NY + y, me)).start()
            return carry

        lax.fori_loop(1, NY, step, 0)

    to_pair = remote(tap_param, taps.at[mz, my], 0, (pair, me))
    to_pair.start()
    loads[0].wait()
    loads[1].wait()
    mix_send[...] = (v_val[...] * v_gate[...]).reshape(NB, CPD, LANES)
    mix[me] = mix_send[me]
    spread(lambda p: (mix_send.at[p], mix.at[me]), 1)
    spread_y(lambda y: (tap_param, taps.at[mz, my]), 2)
    spread(lambda p: (out_gate.at[0, rows(p)], gate.at[me]), 3)
    spread(lambda p: (target.at[0, rows(p)], goal.at[me]), 4)
    to_pair.wait()
    spread_y(lambda y: (taps.at[1 - mz, my], taps.at[1 - mz, my]), 5)
    for load in loads[2:]:
        load.wait()

    lane_args = (tcos, tsin, w_hi, w_lo)
    whole(mix.at[pl.ds(0, NB - 1)], 1).wait()
    mix_spec = forward(mix[...], *lane_args)
    whole(taps.at[0, pl.ds(0, NY - 1)], 2).wait()
    whole(taps.at[0, pl.ds(0, NY - 1)], 5).wait()
    tap_all = taps[...].reshape(2 * NY, CPD, TAPS)
    tap_all = jnp.stack([tap_all[:, :, :LANES], tap_all[:, :, LANES:]], axis=1).reshape(NB, CPD, LANES)
    tap_spec = forward(tap_all * (SEQ**-0.5 / SEQ), *lane_args)
    product = (
        mix_spec[0] * tap_spec[0] - mix_spec[1] * tap_spec[1],
        mix_spec[0] * tap_spec[1] + mix_spec[1] * tap_spec[0],
    )
    row = lax.broadcasted_iota(jnp.int32, (CPD, LANES), 0)
    skip_tile = jnp.zeros((CPD, LANES), jnp.float32)
    for c in range(CPD):
        skip_tile = jnp.where(row == c, skip[me * CPD + c], skip_tile)
    conv[...] = inverse(*product, *lane_args) + skip_tile * mix[...]

    whole(gate.at[pl.ds(0, NB - 1)], 3).wait()
    whole(goal.at[pl.ds(0, NB - 1)], 4).wait()
    grad_out = gate[...] * (gate[...] * conv[...] - goal[...])
    conv[...] = grad_out
    grad_spec = forward(grad_out, *lane_args)

    tap_part = inverse(*conj_mul(grad_spec, mix_spec), *lane_args).reshape(2, NY, 2, CPD, LANES)
    for z in range(2):
        for half in range(2):
            tap_send[:, z, :, half * LANES : (half + 1) * LANES] = tap_part[z, :, half]
    tap_recv[my] = tap_send[my]
    spread_y(lambda y: (tap_send.at[y], tap_recv.at[my]), 6)

    back_send[...] = inverse(*conj_mul(grad_spec, tap_spec), *lane_args) + skip_tile * conv[...]
    back[me] = back_send[me]
    spread(lambda p: (back_send.at[p], back.at[me]), 7)

    whole(tap_recv.at[pl.ds(0, NY - 1)], 6).wait()
    total = jnp.sum(tap_recv[...], axis=0)
    pair_send[...] = total
    to_pair = remote(pair_send.at[1 - mz], pair_recv, 8, (pair, me))
    to_pair.start()

    whole(back.at[pl.ds(0, NB - 1)], 7).wait()
    grad_values[0] = v_gate[...] * back[...].reshape(NB * CPD, LANES)
    to_pair.wait()
    tap_grad[...] = (pair_send[mz] + pair_recv[...]) * ((SEQ * 2 * NY) ** -0.5 / SEQ)


def body(values, in_gate, out_gate, target, tap_param, skip):
    f32, bf16 = jnp.float32, jnp.bfloat16
    block = (NB, CPD, LANES)
    hbm = pl.BlockSpec(memory_space=pl.ANY)
    vmem = pl.BlockSpec(memory_space=pltpu.VMEM)
    constants = [jnp.asarray(t) for t in tables()]
    return pl.pallas_call(
        kernel,
        out_shape=(jax.ShapeDtypeStruct(values.shape, f32), jax.ShapeDtypeStruct(tap_param.shape, f32)),
        in_specs=[hbm] * 5 + [pl.BlockSpec(memory_space=pltpu.SMEM)] + [hbm] * 4,
        out_specs=(vmem, vmem),
        scratch_shapes=[
            pltpu.VMEM((NB * CPD, LANES), f32),
            pltpu.VMEM((NB * CPD, LANES), f32),
            pltpu.VMEM((NB, 1, LANES), f32),
            pltpu.VMEM((NB, 1, LANES), f32),
            pltpu.VMEM((2 * LANES, 2 * LANES), bf16),
            pltpu.VMEM((2 * LANES, 2 * LANES), bf16),
            pltpu.VMEM(block, f32),
            pltpu.VMEM(block, f32),
            pltpu.VMEM(block, f32),
            pltpu.VMEM(block, f32),
            pltpu.VMEM((2, NY, CPD, TAPS), f32),
            pltpu.VMEM(block, f32),
            pltpu.VMEM(block, f32),
            pltpu.VMEM(block, f32),
            pltpu.VMEM((NY, 2, CPD, TAPS), f32),
            pltpu.VMEM((NY, 2, CPD, TAPS), f32),
            pltpu.VMEM((2, CPD, TAPS), f32),
            pltpu.VMEM((CPD, TAPS), f32),
            pltpu.SemaphoreType.DMA((9,)),
            pltpu.SemaphoreType.DMA((9,)),
            pltpu.SemaphoreType.DMA((9,)),
        ],
        compiler_params=pltpu.CompilerParams(collective_id=0, has_side_effects=True, vmem_limit_bytes=60 * 1024 * 1024),
        cost_estimate=pl.CostEstimate(flops=2**30, bytes_accessed=2**20, transcendentals=0),
        name="gated_conv",
    )(values, in_gate, out_gate, target, tap_param, skip, *constants)


def solution(mesh):
    stream = P("dp", None, "context")
    return jax.shard_map(
        body,
        mesh=mesh,
        in_specs=(stream, stream, stream, stream, P("context", "dp"), P()),
        out_specs=(stream, P("context", "dp")),
        check_vma=False,
    )
```

time: 403 us -> 42.2 us (0.10)
  waiting for transfers between devices: 210 us -> 0 us
  blocking collectives: 81.9 us -> 0 us
  other arithmetic: 46.7 us -> 0 us
  Pallas kernels: 0 us -> 39.3 us
  local copies, waits for them, and re-layouts: 25.2 us -> 2.18 us
  starting transfers between devices: 16.4 us -> 0 us
  between operations: 14.8 us -> 0.65 us
  matrix products: 7.33 us -> 0 us
    reduce_scatter x1 -> x0, waiting for transfers between devices: 204 us -> none  [body(): lax.psum_scatter(tap_local, 'dp', scatter_dimension=1, tiled=True)]
    all_gather x1 -> x0, blocking collectives: 55.7 us -> none  [body(): taps_full = lax.all_gather(tap_param, 'dp', axis=1, tiled=True)]
    pallas_call x0 -> x1, Pallas kernels: none -> 39.3 us  [body(): pl.pallas_call(kernel, out_shape=(jax.ShapeDtypeStruct(values.shape, f32)...]
    unnamed x2 -> x0, other arithmetic: 38.5 us -> none
    all_to_all x2 -> x0, blocking collectives: 26.2 us -> none  [the longest x1 13.9 us: body(): lax.all_to_all(conv, 'context', split_axis=2, concat_axis=1, tiled=True)]
    all_to_all x2 -> x0, starting transfers between devices: 16.1 us -> none  [the longest x1 10.4 us: body(): lax.all_to_all(mixed, 'context', split_axis=1, concat_axis=2, tiled=True)]
    unnamed x43 -> x4, local copies, waits for them, and re-layouts: 13.9 us -> 2.18 us
    dot_general x12 -> x0, matrix products: 7.33 us -> none  [matmul_high(): return jnp.matmul(left, right, precision=lax.Precision.HIGHEST)]
  transfers between devices with their start and end apart: 3 -> 0, of which waited for: 2 -> 0; matrix products, arithmetic and copies ran while one was open for 3% -> 0% of each run, Pallas kernels for 0% -> 0%
where the time goes in v1:
time: 42.2 us; the launch traced here: 42.1 us
  Pallas kernels  39.3 us (93%)
  local copies, waits for them, and re-layouts  2.18 us (5%)
  between operations  0.65 us (2%)
    pallas_call x1, Pallas kernels, body(): pl.pallas_call(kernel, out_shape=(jax.ShapeDtypeStruct(values.shape, f32)...  39.3 us
    unnamed x4, local copies, waits for them, and re-layouts  2.18 us

profile of v1, /device:TPU:6, one launch (start us, length us, event | category | flops | bytes accessed | tf_op | source)
XLA Modules:
  0.0 42.1 jit_solution(12824854748565203770)
XLA Ops:
  0.6 39.3 %gated_conv.1 = (f32[1,256,128]{2,1,0:T(8,128)}, f32[8,256]{1,0:T(8,128)}) custom-call(f32[1,256,128]{2,1,0:T(8,128)} %values.1, f32[1,256,128]{2,1,0:T(8,128)} %in_gate.1, f32[1,256,128]{2,1,0:T(8,128)} %out_gate.1, f32[1,256,128]{2,1,0:T(8,128)} %target.1, f32[8,256]{1,0:T(8,128)} %tap_param.1, f32[256]{0:T(256)} %skip.1, ...), custom_call_target="tpu_custom_call" | custom-call | flops 1073741824 | bytes 1048576 | tf_op jit(solution)/shard_map/gated_conv/pallas_call | solution.py:241
  39.9 0.0 copy-start
  39.9 1.6 %copy.14 = f32[1,256,128]{2,1,0:T(8,128)} copy(f32[1,256,128]{2,1,0:T(8,128)} %get-tuple-element.4) | data formatting | bytes 262144
  41.5 0.0 copy-done
  41.5 0.6 %copy.15 = f32[8,256]{1,0:T(8,128)} copy(f32[8,256]{1,0:T(8,128)S(1)} %copy-done) | data formatting | bytes 16384
Async XLA Ops:
  39.9 1.6 %copy-start = (f32[8,256]{1,0:T(8,128)S(1)}, f32[8,256]{1,0:T(8,128)}, u32[]{:S(2)}) copy-start(f32[8,256]{1,0:T(8,128)} %get-tuple-element.5) | copy-start | bytes 24580

commit v2 on v1

v2 whole, which is shorter than its diff:
```python
import functools
import math

import jax
import jax.numpy as jnp
import numpy as np
from jax import lax
from jax.experimental import pallas as pl
from jax.experimental.pallas import tpu as pltpu
from jax.sharding import PartitionSpec as P

MESH = pl.DeviceIdType.MESH
NB = 32
LANES = 128
CPD = 8
NY = 8
SEQ = NB * LANES
TAPS = 2 * LANES


def leaf_angles(theta, length):
    if length == 1:
        return [theta]
    return leaf_angles(theta / 2, length // 2) + leaf_angles(theta / 2 + math.pi, length // 2)


@functools.cache
def tables():
    order = np.array([round((a * 64 / (2 * math.pi) - 0.5) / 2) % NB for a in leaf_angles(math.pi / 2, NB)])
    r = np.arange(LANES)
    angle = 2 * math.pi * (2 * order[:, None] + 0.5) * r[None, :] / (2 * SEQ)
    turn = 2 * math.pi * (r[:, None] * r[None, :] % LANES) / LANES
    c, s = np.cos(turn), np.sin(turn)
    w = np.block([[c, -s], [s, c]]).astype(np.float32)
    w_hi = w.astype(jnp.bfloat16)
    w_lo = (w - w_hi.astype(np.float32)).astype(jnp.bfloat16)
    return (
        np.cos(angle).astype(np.float32)[:, None, :],
        np.sin(angle).astype(np.float32)[:, None, :],
        w_hi,
        w_lo,
    )


def evaluate(re, im, theta):
    length = re.shape[0]
    if length == 1:
        return [(re, im)]
    half = length // 2
    c, s = math.cos(theta / 2), math.sin(theta / 2)
    if im is None:
        t_re, t_im = c * re[half:], -s * re[half:]
        low = (re[:half] + t_re, t_im)
        high = (re[:half] - t_re, -t_im)
    else:
        t_re = c * re[half:] + s * im[half:]
        t_im = c * im[half:] - s * re[half:]
        low = (re[:half] + t_re, im[:half] + t_im)
        high = (re[:half] - t_re, im[:half] - t_im)
    return evaluate(*low, theta / 2) + evaluate(*high, theta / 2 + math.pi)


def gather_back(re, im, theta, real_only):
    length = re.shape[0]
    if length == 1:
        return re, im
    half = length // 2
    a_re, a_im = gather_back(re[:half], im[:half], theta / 2, False)
    b_re, b_im = gather_back(re[half:], im[half:], theta / 2 + math.pi, False)
    c, s = math.cos(theta / 2), math.sin(theta / 2)
    d_re, d_im = a_re - b_re, a_im - b_im
    top = c * d_re - s * d_im
    if real_only:
        return jnp.concatenate([a_re + b_re, top], axis=0), None
    return jnp.concatenate([a_re + b_re, top], axis=0), jnp.concatenate([a_im + b_im, c * d_im + s * d_re], axis=0)


def lane_transform(left, right, w_hi, w_lo):
    joined = jnp.concatenate([left, right], axis=1)
    hi = joined.astype(jnp.bfloat16)
    lo = (joined - hi.astype(jnp.float32)).astype(jnp.bfloat16)
    dot = functools.partial(jnp.dot, preferred_element_type=jnp.float32)
    out = dot(hi, w_hi[...]) + (dot(lo, w_hi[...]) + dot(hi, w_lo[...]))
    return out[:, :LANES], out[:, LANES:]


def forward(x, tcos, tsin, w_hi, w_lo):
    leaves = evaluate(x, None, math.pi / 2)
    re = jnp.concatenate([leaf[0] for leaf in leaves], axis=0)
    im = jnp.concatenate([leaf[1] for leaf in leaves], axis=0)
    c, s = tcos[...], tsin[...]
    flat = (NB * CPD, LANES)
    return lane_transform((re * c + im * s).reshape(flat), (im * c - re * s).reshape(flat), w_hi, w_lo)


def inverse(re, im, tcos, tsin, w_hi, w_lo):
    b_im, b_re = lane_transform(im, re, w_hi, w_lo)
    b_im, b_re = b_im.reshape(NB, CPD, LANES), b_re.reshape(NB, CPD, LANES)
    c, s = tcos[...], tsin[...]
    return gather_back(b_re * c - b_im * s, b_im * c + b_re * s, math.pi / 2, True)[0]


def conj_mul(a, b):
    return a[0] * b[0] + a[1] * b[1], a[1] * b[0] - a[0] * b[1]


def kernel(
    values, in_gate, out_gate, target, tap_param, skip, tcos_h, tsin_h, whi_h, wlo_h,
    back, tap_a, tap_b,
    v_val, v_gate, tcos, tsin, w_hi, w_lo,
    mix_send, mix, goal_send, goal, taps, grad, back_send, tap_send, tap_recv, pair_send,
    load_sem, send_sem, recv_sem,
):
    me_d, me = lax.axis_index("dp"), lax.axis_index("context")
    mz, my = me_d // NY, me_d % NY
    low, side, core = me // 8, me % 8 // 2, me % 2
    other = (1 - mz) * NY + my
    owned = (me + NB // 2) % NB
    barrier = pltpu.get_barrier_semaphore()

    def partner(j):
        flip = 3 - j // 8
        z = (low // 2 + flip // 2) % 2 * 2 + (low % 2 + flip % 2) % 2
        return z * 8 + (side + 3 - j % 8 // 2) % 4 * 2 + (core + 1 - j % 2) % 2

    def partner_y(k):
        half = k // 2
        return (my + 4 + (1 - k % 2) * half - k % 2 * (half + 1)) % NY

    def greet(j, carry):
        pl.semaphore_signal(barrier, inc=1, device_id=(me_d, partner(j)), device_id_type=MESH)
        return carry

    def greet_y(k, carry):
        pl.semaphore_signal(barrier, inc=1, device_id=(mz * NY + partner_y(k), me), device_id_type=MESH)
        return carry

    lax.fori_loop(0, NY - 1, greet_y, 0)
    pl.semaphore_signal(barrier, inc=1, device_id=(other, owned), device_id_type=MESH)
    lax.fori_loop(0, NB - 1, greet, 0)

    loads = [
        (values, v_val),
        (in_gate, v_gate),
        (out_gate, goal_send.at[:, 0]),
        (target, goal_send.at[:, 1]),
        (tcos_h, tcos),
        (tsin_h, tsin),
        (whi_h, w_hi),
        (wlo_h, w_lo),
    ]
    loads = [pltpu.make_async_copy(src, dst, load_sem.at[k]) for k, (src, dst) in enumerate(loads)]
    for load in loads:
        load.start()
    for load in loads[:2]:
        load.wait()
    mix_send[...] = v_val[...] * v_gate[...]
    for load in loads[2:4]:
        load.wait()
    pl.semaphore_wait(barrier, NB - 1 + NY - 1 + 1)

    def remote(src, dst, k, device):
        return pltpu.make_async_remote_copy(
            src_ref=src, dst_ref=dst, send_sem=send_sem.at[k], recv_sem=recv_sem.at[k], device_id=device, device_id_type=MESH
        )

    def whole(ref, k):
        return remote(ref, ref, k, (other, me))

    def spread(make, k):
        def step(j, carry):
            p = partner(j)
            src, dst = make(p)
            remote(src, dst, k, (me_d, p)).start()
            return carry

        lax.fori_loop(0, NB - 1, step, 0)

    def spread_y(make, k):
        def step(j, carry):
            y = partner_y(j)
            src, dst = make(y)
            remote(src, dst, k, (mz * NY + y, me)).start()
            return carry

        lax.fori_loop(0, NY - 1, step, 0)

    for z in range(2):
        remote(tap_param, taps.at[my, mz], 0, (z * NY + my, owned)).start()
    spread(lambda p: (mix_send.at[(p + NB // 2) % NB], mix.at[me]), 1)
    whole(taps.at[my], 0).wait()
    spread_y(lambda y: (taps.at[my], taps.at[my]), 2)
    spread(lambda p: (goal_send.at[(p + NB // 2) % NB], goal.at[me]), 7)
    mix[me] = mix_send[owned]
    goal[me] = goal_send[owned]
    for load in loads[4:]:
        load.wait()

    row = lax.broadcasted_iota(jnp.int32, (CPD, LANES), 0)
    skip_tile = jnp.zeros((CPD, LANES), jnp.float32)
    for c in range(CPD):
        skip_tile = jnp.where(row == c, skip[owned * CPD + c], skip_tile)

    lane_args = (tcos, tsin, w_hi, w_lo)
    whole(mix.at[pl.ds(0, NB - 1)], 1).wait()
    mixed = mix[...]
    mix_spec = forward(mixed, *lane_args)
    whole(taps.at[pl.ds(0, NY - 1)], 2).wait()
    tap_all = jnp.concatenate([taps[:, 0], taps[:, 1]], axis=0)
    tap_all = jnp.stack([tap_all[:, :, :LANES], tap_all[:, :, LANES:]], axis=1).reshape(NB, CPD, LANES)
    tap_spec = forward(tap_all * (SEQ**-0.5 / SEQ), *lane_args)
    product = (
        mix_spec[0] * tap_spec[0] - mix_spec[1] * tap_spec[1],
        mix_spec[0] * tap_spec[1] + mix_spec[1] * tap_spec[0],
    )
    grad[...] = inverse(*product, *lane_args) + skip_tile * mixed

    whole(goal.at[pl.ds(0, NB - 1)], 7).wait()
    gate = goal[:, 0]
    grad_out = gate * (gate * grad[...] - goal[:, 1])
    grad[...] = grad_out
    grad_spec = forward(grad_out, *lane_args)

    tap_part = inverse(*conj_mul(grad_spec, mix_spec), *lane_args).reshape(2, NY, 2, CPD, LANES)
    for z in range(2):
        for half in range(2):
            tap_send[:, z, :, half * LANES : (half + 1) * LANES] = tap_part[z, :, half]
    spread_y(lambda y: (tap_send.at[y], tap_recv.at[my]), 4)
    tap_recv[my] = tap_send[my]

    back_send[...] = inverse(*conj_mul(grad_spec, tap_spec), *lane_args) + skip_tile * grad[...]
    spread(lambda p: (back_send.at[p], back.at[owned]), 5)
    keep = pltpu.make_async_copy(back_send.at[me], back.at[owned], load_sem.at[0])
    keep.start()

    whole(tap_recv.at[pl.ds(0, NY - 1)], 4).wait()
    pair_send[...] = jnp.sum(tap_recv[...], axis=0)
    for z in range(2):

        @pl.when(mz == 0)
        def _():
            remote(pair_send.at[z], tap_a, 3, (z * NY + my, owned)).start()

        @pl.when(mz == 1)
        def _():
            remote(pair_send.at[z], tap_b, 6, (z * NY + my, owned)).start()

    keep.wait()
    whole(back.at[pl.ds(0, NB - 1)], 5).wait()
    whole(tap_a, 3).wait_recv()
    whole(tap_b, 6).wait_recv()

    @pl.when(mz == 0)
    def _():
        whole(pair_send, 3).wait_send()

    @pl.when(mz == 1)
    def _():
        whole(pair_send, 6).wait_send()


def finish_kernel(back, in_gate, tap_a, tap_b, grad_values, tap_grad):
    grad_values[...] = in_gate[...] * back[...]
    tap_grad[...] = (tap_a[...] + tap_b[...]) * ((SEQ * 2 * NY) ** -0.5 / SEQ)


def body(values, in_gate, out_gate, target, tap_param, skip):
    f32, bf16 = jnp.float32, jnp.bfloat16
    block = (NB, CPD, LANES)
    shape = values.shape
    hbm = pl.BlockSpec(memory_space=pl.ANY)
    vmem = pl.BlockSpec(memory_space=pltpu.VMEM)
    constants = [jnp.asarray(t) for t in tables()]
    values, in_gate, out_gate, target = [a.reshape(block) for a in (values, in_gate, out_gate, target)]
    tap_shape = jax.ShapeDtypeStruct(tap_param.shape, f32)
    back, tap_a, tap_b = pl.pallas_call(
        kernel,
        out_shape=(jax.ShapeDtypeStruct(block, f32), tap_shape, tap_shape),
        in_specs=[hbm] * 5 + [pl.BlockSpec(memory_space=pltpu.SMEM)] + [hbm] * 4,
        out_specs=(hbm, hbm, hbm),
        scratch_shapes=[
            pltpu.VMEM(block, f32),
            pltpu.VMEM(block, f32),
            pltpu.VMEM((NB, 1, LANES), f32),
            pltpu.VMEM((NB, 1, LANES), f32),
            pltpu.VMEM((2 * LANES, 2 * LANES), bf16),
            pltpu.VMEM((2 * LANES, 2 * LANES), bf16),
            pltpu.VMEM(block, f32),
            pltpu.VMEM(block, f32),
            pltpu.VMEM((NB, 2, CPD, LANES), f32),
            pltpu.VMEM((NB, 2, CPD, LANES), f32),
            pltpu.VMEM((NY, 2, CPD, TAPS), f32),
            pltpu.VMEM(block, f32),
            pltpu.VMEM(block, f32),
            pltpu.VMEM((NY, 2, CPD, TAPS), f32),
            pltpu.VMEM((NY, 2, CPD, TAPS), f32),
            pltpu.VMEM((2, CPD, TAPS), f32),
            pltpu.SemaphoreType.DMA((8,)),
            pltpu.SemaphoreType.DMA((8,)),
            pltpu.SemaphoreType.DMA((8,)),
        ],
        compiler_params=pltpu.CompilerParams(collective_id=0, has_side_effects=True, vmem_limit_bytes=56 * 1024 * 1024),
        cost_estimate=pl.CostEstimate(flops=2**30, bytes_accessed=2**20, transcendentals=0),
        name="gated_conv",
    )(values, in_gate, out_gate, target, tap_param, skip, *constants)
    grad_values, tap_grad = pl.pallas_call(
        finish_kernel,
        out_shape=(jax.ShapeDtypeStruct(block, f32), tap_shape),
        in_specs=[vmem] * 4,
        out_specs=(vmem, vmem),
        name="finish",
    )(back, in_gate, tap_a, tap_b)
    return grad_values.reshape(shape), tap_grad


def solution(mesh):
    stream = P("dp", None, "context")
    return jax.shard_map(
        body,
        mesh=mesh,
        in_specs=(stream, stream, stream, stream, P("context", "dp"), P()),
        out_specs=(stream, P("context", "dp")),
        check_vma=False,
    )
```

time: 42.2 us -> 39.5 us (0.936)
  the two profiles are of different devices: /device:TPU:6 before, /device:TPU:64 now
where the time goes in v2:
time: 39.5 us; the launch traced here: 39.3 us
  Pallas kernels  38.6 us (98%)
  between operations  0.64 us (2%)
    pallas_call x1, Pallas kernels, body(): pl.pallas_call(kernel, out_shape=(jax.ShapeDtypeStruct(block, f32), tap_s...  37 us
    pallas_call x1, Pallas kernels, body(): pl.pallas_call(finish_kernel, out_shape=(jax.ShapeDtypeStruct(block, f32)...  1.65 us

profile of v2, /device:TPU:64, one launch (start us, length us, event | category | flops | bytes accessed | tf_op | source)
XLA Modules:
  0.0 39.3 jit_solution(4814956514340770801)
XLA Ops:
  0.6 37.0 %gated_conv.1 = (f32[32,8,128]{2,1,0:T(8,128)}, f32[8,256]{1,0:T(8,128)}, f32[8,256]{1,0:T(8,128)}) custom-call(f32[32,8,128]{2,1,0:T(8,128)} %bitcast.7, f32[32,8,128]{2,1,0:T(8,128)} %bitcast.5, f32[32,8,128]{2,1,0:T(8,128)} %bitcast.8, f32[32,8,128]{2,1,0:T(8,128)} %bitcast.9, f32[8,256]{1,0:T(8,128)} %tap_param.1, f32[256]{0:T(256)} %skip.1, ...), custom_call_target="tpu_custom_call" | custom-call | flops 1073741824 | bytes 1048576 | tf_op jit(solution)/shard_map/gated_conv/pallas_call | solution.py:276
  37.6 1.6 %finish.1 = (f32[32,8,128]{2,1,0:T(8,128)}, f32[8,256]{1,0:T(8,128)}) custom-call(f32[32,8,128]{2,1,0:T(8,128)} %get-tuple-element.7.back, f32[32,8,128]{2,1,0:T(8,128)} %bitcast.6, f32[8,256]{1,0:T(8,128)} %get-tuple-element.8.tap_a, f32[8,256]{1,0:T(8,128)} %get-tuple-element.9.tap_b), custom_call_target="tpu_custom_call" | custom-call | tf_op jit(solution)/shard_map/finish/pallas_call | solution.py:306

commit v3 on v2

--- a/solution.py
+++ b/solution.py
@@ -106,26 +106,25 @@
 
 def kernel(
     values, in_gate, out_gate, target, tap_param, skip, tcos_h, tsin_h, whi_h, wlo_h,
-    back, tap_a, tap_b,
-    v_val, v_gate, tcos, tsin, w_hi, w_lo,
-    mix_send, mix, goal_send, goal, taps, grad, back_send, tap_send, tap_recv, pair_send,
+    back, tap_parts,
+    v_val, v_gate, tcos, tsin, w_hi, w_lo, tap_block,
+    mix_send, mix, goal_send, goal, taps, grad, back_send, tap_send,
     load_sem, send_sem, recv_sem,
 ):
     me_d, me = lax.axis_index("dp"), lax.axis_index("context")
     mz, my = me_d // NY, me_d % NY
-    low, side, core = me // 8, me % 8 // 2, me % 2
     other = (1 - mz) * NY + my
     owned = (me + NB // 2) % NB
     barrier = pltpu.get_barrier_semaphore()
 
     def partner(j):
-        flip = 3 - j // 8
-        z = (low // 2 + flip // 2) % 2 * 2 + (low % 2 + flip % 2) % 2
-        return z * 8 + (side + 3 - j % 8 // 2) % 4 * 2 + (core + 1 - j % 2) % 2
+        return lax.rem(me + 1 + j, NB)
+
+    def turn(p):
+        return lax.rem(p + NB // 2, NB)
 
     def partner_y(k):
-        half = k // 2
-        return (my + 4 + (1 - k % 2) * half - k % 2 * (half + 1)) % NY
+        return lax.rem(my + 4 + k + (k > 3), NY)
 
     def greet(j, carry):
         pl.semaphore_signal(barrier, inc=1, device_id=(me_d, partner(j)), device_id_type=MESH)
@@ -148,15 +147,11 @@
         (tsin_h, tsin),
         (whi_h, w_hi),
         (wlo_h, w_lo),
+        (tap_param, tap_block),
     ]
     loads = [pltpu.make_async_copy(src, dst, load_sem.at[k]) for k, (src, dst) in enumerate(loads)]
-    for load in loads:
+    for load in loads[-1:] + loads[:-1]:
         load.start()
-    for load in loads[:2]:
-        load.wait()
-    mix_send[...] = v_val[...] * v_gate[...]
-    for load in loads[2:4]:
-        load.wait()
     pl.semaphore_wait(barrier, NB - 1 + NY - 1 + 1)
 
     def remote(src, dst, k, device):
@@ -185,15 +180,33 @@
 
         lax.fori_loop(0, NY - 1, step, 0)
 
-    for z in range(2):
-        remote(tap_param, taps.at[my, mz], 0, (z * NY + my, owned)).start()
-    spread(lambda p: (mix_send.at[(p + NB // 2) % NB], mix.at[me]), 1)
-    whole(taps.at[my], 0).wait()
-    spread_y(lambda y: (taps.at[my], taps.at[my]), 2)
-    spread(lambda p: (goal_send.at[(p + NB // 2) % NB], goal.at[me]), 7)
+    loads[8].wait()
+
+
+    @pl.when(mz == 0)
+    def _():
+        for z in range(2):
+            remote(tap_block, taps.at[0, my], 6 * z, (z * NY + my, owned)).start()
+
+    @pl.when(mz == 1)
+    def _():
+        for z in range(2):
+            remote(tap_block, taps.at[1, my], 6 - 6 * z, (z * NY + my, owned)).start()
+
+    for load in loads[:2]:
+        load.wait()
+    mix_send[...] = v_val[...] * v_gate[...]
+    for load in loads[2:4]:
+        load.wait()
+    spread(lambda p: (mix_send.at[turn(p)], mix.at[me]), 1)
+    whole(taps.at[mz, my], 0).wait()
+    spread_y(lambda y: (taps.at[mz, my], taps.at[mz, my]), 2)
+    spread(lambda p: (goal_send.at[turn(p)], goal.at[me]), 7)
+    whole(taps.at[1 - mz, my], 6).wait()
+    spread_y(lambda y: (taps.at[1 - mz, my], taps.at[1 - mz, my]), 3)
     mix[me] = mix_send[owned]
     goal[me] = goal_send[owned]
-    for load in loads[4:]:
+    for load in loads[4:8]:
         load.wait()
 
     row = lax.broadcasted_iota(jnp.int32, (CPD, LANES), 0)
@@ -205,8 +218,9 @@
     whole(mix.at[pl.ds(0, NB - 1)], 1).wait()
     mixed = mix[...]
     mix_spec = forward(mixed, *lane_args)
-    whole(taps.at[pl.ds(0, NY - 1)], 2).wait()
-    tap_all = jnp.concatenate([taps[:, 0], taps[:, 1]], axis=0)
+    whole(taps.at[0, pl.ds(0, NY - 1)], 2).wait()
+    whole(taps.at[0, pl.ds(0, NY - 1)], 3).wait()
+    tap_all = taps[...].reshape(2 * NY, CPD, TAPS)
     tap_all = jnp.stack([tap_all[:, :, :LANES], tap_all[:, :, LANES:]], axis=1).reshape(NB, CPD, LANES)
     tap_spec = forward(tap_all * (SEQ**-0.5 / SEQ), *lane_args)
     product = (
@@ -221,47 +235,43 @@
     grad[...] = grad_out
     grad_spec = forward(grad_out, *lane_args)
 
+    def spread_lags(z):
+        def step(k, carry):
+            y = lax.rem(my + 4 + k, NY)
+            remote(tap_send.at[y, z], tap_parts.at[me_d], 4, (z * NY + y, owned)).start()
+            return carry
+
+        lax.fori_loop(0, NY, step, 0)
+
     tap_part = inverse(*conj_mul(grad_spec, mix_spec), *lane_args).reshape(2, NY, 2, CPD, LANES)
     for z in range(2):
         for half in range(2):
             tap_send[:, z, :, half * LANES : (half + 1) * LANES] = tap_part[z, :, half]
-    spread_y(lambda y: (tap_send.at[y], tap_recv.at[my]), 4)
-    tap_recv[my] = tap_send[my]
 
     back_send[...] = inverse(*conj_mul(grad_spec, tap_spec), *lane_args) + skip_tile * grad[...]
+
+    @pl.when(mz == 1)
+    def _():
+        spread_lags(0)
+
     spread(lambda p: (back_send.at[p], back.at[owned]), 5)
+
+    @pl.when(mz == 0)
+    def _():
+        spread_lags(0)
+
+    spread_lags(1)
     keep = pltpu.make_async_copy(back_send.at[me], back.at[owned], load_sem.at[0])
     keep.start()
 
-    whole(tap_recv.at[pl.ds(0, NY - 1)], 4).wait()
-    pair_send[...] = jnp.sum(tap_recv[...], axis=0)
-    for z in range(2):
-
-        @pl.when(mz == 0)
-        def _():
-            remote(pair_send.at[z], tap_a, 3, (z * NY + my, owned)).start()
-
-        @pl.when(mz == 1)
-        def _():
-            remote(pair_send.at[z], tap_b, 6, (z * NY + my, owned)).start()
-
+    whole(tap_parts, 4).wait()
     keep.wait()
     whole(back.at[pl.ds(0, NB - 1)], 5).wait()
-    whole(tap_a, 3).wait_recv()
-    whole(tap_b, 6).wait_recv()
-
-    @pl.when(mz == 0)
-    def _():
-        whole(pair_send, 3).wait_send()
-
-    @pl.when(mz == 1)
-    def _():
-        whole(pair_send, 6).wait_send()
-
-
-def finish_kernel(back, in_gate, tap_a, tap_b, grad_values, tap_grad):
+
+
+def finish_kernel(back, in_gate, tap_parts, grad_values, tap_grad):
     grad_values[...] = in_gate[...] * back[...]
-    tap_grad[...] = (tap_a[...] + tap_b[...]) * ((SEQ * 2 * NY) ** -0.5 / SEQ)
+    tap_grad[...] = jnp.sum(tap_parts[...], axis=0) * ((SEQ * 2 * NY) ** -0.5 / SEQ)
 
 
 def body(values, in_gate, out_gate, target, tap_param, skip):
@@ -273,11 +283,11 @@
     constants = [jnp.asarray(t) for t in tables()]
     values, in_gate, out_gate, target = [a.reshape(block) for a in (values, in_gate, out_gate, target)]
     tap_shape = jax.ShapeDtypeStruct(tap_param.shape, f32)
-    back, tap_a, tap_b = pl.pallas_call(
+    back, tap_parts = pl.pallas_call(
         kernel,
-        out_shape=(jax.ShapeDtypeStruct(block, f32), tap_shape, tap_shape),
+        out_shape=(jax.ShapeDtypeStruct(block, f32), jax.ShapeDtypeStruct((2 * NY, CPD, TAPS), f32)),
         in_specs=[hbm] * 5 + [pl.BlockSpec(memory_space=pltpu.SMEM)] + [hbm] * 4,
-        out_specs=(hbm, hbm, hbm),
+        out_specs=(hbm, hbm),
         scratch_shapes=[
             pltpu.VMEM(block, f32),
             pltpu.VMEM(block, f32),
@@ -285,17 +295,16 @@
             pltpu.VMEM((NB, 1, LANES), f32),
             pltpu.VMEM((2 * LANES, 2 * LANES), bf16),
             pltpu.VMEM((2 * LANES, 2 * LANES), bf16),
+            pltpu.VMEM((CPD, TAPS), f32),
             pltpu.VMEM(block, f32),
             pltpu.VMEM(block, f32),
             pltpu.VMEM((NB, 2, CPD, LANES), f32),
             pltpu.VMEM((NB, 2, CPD, LANES), f32),
+            pltpu.VMEM((2, NY, CPD, TAPS), f32),
+            pltpu.VMEM(block, f32),
+            pltpu.VMEM(block, f32),
             pltpu.VMEM((NY, 2, CPD, TAPS), f32),
-            pltpu.VMEM(block, f32),
-            pltpu.VMEM(block, f32),
-            pltpu.VMEM((NY, 2, CPD, TAPS), f32),
-            pltpu.VMEM((NY, 2, CPD, TAPS), f32),
-            pltpu.VMEM((2, CPD, TAPS), f32),
-            pltpu.SemaphoreType.DMA((8,)),
+            pltpu.SemaphoreType.DMA((9,)),
             pltpu.SemaphoreType.DMA((8,)),
             pltpu.SemaphoreType.DMA((8,)),
         ],
@@ -306,10 +315,10 @@
     grad_values, tap_grad = pl.pallas_call(
         finish_kernel,
         out_shape=(jax.ShapeDtypeStruct(block, f32), tap_shape),
-        in_specs=[vmem] * 4,
+        in_specs=[vmem] * 3,
         out_specs=(vmem, vmem),
         name="finish",
-    )(back, in_gate, tap_a, tap_b)
+    )(back, in_gate, tap_parts)
     return grad_values.reshape(shape), tap_grad
 
 

time: 39.5 us -> 36 us (0.911)
  the two profiles are of different devices: /device:TPU:64 before, /device:TPU:6 now
where the time goes in v3:
time: 36 us; the launch traced here: 35.6 us
  Pallas kernels  35 us (97%)
  between operations  0.64 us (2%)
    pallas_call x1, Pallas kernels, body(): pl.pallas_call(kernel, out_shape=(jax.ShapeDtypeStruct(block, f32), jax.S...  33.3 us
    pallas_call x1, Pallas kernels, body(): pl.pallas_call(finish_kernel, out_shape=(jax.ShapeDtypeStruct(block, f32)...  1.7 us

profile of v3, /device:TPU:6, one launch (start us, length us, event | category | flops | bytes accessed | tf_op | source)
XLA Modules:
  0.0 35.6 jit_solution(3752435484935373470)
XLA Ops:
  0.6 33.3 %gated_conv.1 = (f32[32,8,128]{2,1,0:T(8,128)}, f32[16,8,256]{2,1,0:T(8,128)}) custom-call(f32[32,8,128]{2,1,0:T(8,128)} %bitcast.7, f32[32,8,128]{2,1,0:T(8,128)} %bitcast.5, f32[32,8,128]{2,1,0:T(8,128)} %bitcast.8, f32[32,8,128]{2,1,0:T(8,128)} %bitcast.9, f32[8,256]{1,0:T(8,128)} %tap_param.1, f32[256]{0:T(256)} %skip.1, ...), custom_call_target="tpu_custom_call" | custom-call | flops 1073741824 | bytes 1048576 | tf_op jit(solution)/shard_map/gated_conv/pallas_call | solution.py:286
  33.9 1.7 %finish.1 = (f32[32,8,128]{2,1,0:T(8,128)}, f32[8,256]{1,0:T(8,128)}) custom-call(f32[32,8,128]{2,1,0:T(8,128)} %get-tuple-element.6.back, f32[32,8,128]{2,1,0:T(8,128)} %bitcast.6, f32[16,8,256]{2,1,0:T(8,128)} %get-tuple-element.7.tap_parts), custom_call_target="tpu_custom_call" | custom-call | tf_op jit(solution)/shard_map/finish/pallas_call | solution.py:315

commit v4 on v3

--- a/solution.py
+++ b/solution.py
@@ -237,7 +237,7 @@
 
     def spread_lags(z):
         def step(k, carry):
-            y = lax.rem(my + 4 + k, NY)
+            y = k
             remote(tap_send.at[y, z], tap_parts.at[me_d], 4, (z * NY + y, owned)).start()
             return carry
 
@@ -254,7 +254,17 @@
     def _():
         spread_lags(0)
 
-    spread(lambda p: (back_send.at[p], back.at[owned]), 5)
+
+    def spread_back(j, carry):
+        p = lax.div(j, 8) * 8 + lax.rem(me + 1 + j, 8)
+
+        @pl.when(p != me)
+        def _():
+            remote(back_send.at[p], back.at[owned], 5, (me_d, p)).start()
+
+        return carry
+
+    lax.fori_loop(0, NB, spread_back, 0)
 
     @pl.when(mz == 0)
     def _():

time: 36 us -> 35.7 us (level)
  Pallas kernels: 35 us -> 34.6 us
where the time goes in v4:
time: 35.7 us; the launch traced here: 35.3 us
  Pallas kernels  34.6 us (97%)
  between operations  0.64 us (2%)
    pallas_call x1, Pallas kernels, body(): pl.pallas_call(kernel, out_shape=(jax.ShapeDtypeStruct(block, f32), jax.S...  32.9 us
    pallas_call x1, Pallas kernels, body(): pl.pallas_call(finish_kernel, out_shape=(jax.ShapeDtypeStruct(block, f32)...  1.7 us

profile of v4, /device:TPU:6, one launch (start us, length us, event | category | flops | bytes accessed | tf_op | source)
XLA Modules:
  0.0 35.3 jit_solution(12339153246608570216)
XLA Ops:
  0.6 32.9 %gated_conv.1 = (f32[32,8,128]{2,1,0:T(8,128)}, f32[16,8,256]{2,1,0:T(8,128)}) custom-call(f32[32,8,128]{2,1,0:T(8,128)} %bitcast.7, f32[32,8,128]{2,1,0:T(8,128)} %bitcast.5, f32[32,8,128]{2,1,0:T(8,128)} %bitcast.8, f32[32,8,128]{2,1,0:T(8,128)} %bitcast.9, f32[8,256]{1,0:T(8,128)} %tap_param.1, f32[256]{0:T(256)} %skip.1, ...), custom_call_target="tpu_custom_call" | custom-call | flops 1073741824 | bytes 1048576 | tf_op jit(solution)/shard_map/gated_conv/pallas_call | solution.py:296
  33.6 1.7 %finish.1 = (f32[32,8,128]{2,1,0:T(8,128)}, f32[8,256]{1,0:T(8,128)}) custom-call(f32[32,8,128]{2,1,0:T(8,128)} %get-tuple-element.6.back, f32[32,8,128]{2,1,0:T(8,128)} %bitcast.6, f32[16,8,256]{2,1,0:T(8,128)} %get-tuple-element.7.tap_parts), custom_call_target="tpu_custom_call" | custom-call | tf_op jit(solution)/shard_map/finish/pallas_call | solution.py:325

commit v5 on v4

--- a/solution.py
+++ b/solution.py
@@ -196,11 +196,11 @@
     for load in loads[:2]:
         load.wait()
     mix_send[...] = v_val[...] * v_gate[...]
-    for load in loads[2:4]:
-        load.wait()
     spread(lambda p: (mix_send.at[turn(p)], mix.at[me]), 1)
     whole(taps.at[mz, my], 0).wait()
     spread_y(lambda y: (taps.at[mz, my], taps.at[mz, my]), 2)
+    for load in loads[2:4]:
+        load.wait()
     spread(lambda p: (goal_send.at[turn(p)], goal.at[me]), 7)
     whole(taps.at[1 - mz, my], 6).wait()
     spread_y(lambda y: (taps.at[1 - mz, my], taps.at[1 - mz, my]), 3)

time: 35.7 us -> 35.7 us (level)
  no operation moved by 1% of the time
where the time goes in v5:
time: 35.7 us; the launch traced here: 35.2 us
  Pallas kernels  34.6 us (97%)
  between operations  0.64 us (2%)
    pallas_call x1, Pallas kernels, body(): pl.pallas_call(kernel, out_shape=(jax.ShapeDtypeStruct(block, f32), jax.S...  32.9 us
    pallas_call x1, Pallas kernels, body(): pl.pallas_call(finish_kernel, out_shape=(jax.ShapeDtypeStruct(block, f32)...  1.7 us

profile of v5, /device:TPU:6, one launch (start us, length us, event | category | flops | bytes accessed | tf_op | source)
XLA Modules:
  0.0 35.2 jit_solution(5979694571455292737)
XLA Ops:
  0.6 32.9 %gated_conv.1 = (f32[32,8,128]{2,1,0:T(8,128)}, f32[16,8,256]{2,1,0:T(8,128)}) custom-call(f32[32,8,128]{2,1,0:T(8,128)} %bitcast.7, f32[32,8,128]{2,1,0:T(8,128)} %bitcast.5, f32[32,8,128]{2,1,0:T(8,128)} %bitcast.8, f32[32,8,128]{2,1,0:T(8,128)} %bitcast.9, f32[8,256]{1,0:T(8,128)} %tap_param.1, f32[256]{0:T(256)} %skip.1, ...), custom_call_target="tpu_custom_call" | custom-call | flops 1073741824 | bytes 1048576 | tf_op jit(solution)/shard_map/gated_conv/pallas_call | solution.py:296
  33.5 1.7 %finish.1 = (f32[32,8,128]{2,1,0:T(8,128)}, f32[8,256]{1,0:T(8,128)}) custom-call(f32[32,8,128]{2,1,0:T(8,128)} %get-tuple-element.6.back, f32[32,8,128]{2,1,0:T(8,128)} %bitcast.6, f32[16,8,256]{2,1,0:T(8,128)} %get-tuple-element.7.tap_parts), custom_call_target="tpu_custom_call" | custom-call | tf_op jit(solution)/shard_map/finish/pallas_call | solution.py:325
